TPU v7x, 32 devices: a whole 2x2x4 slice. The times are simulated.
32 devices in a mesh: elec: 8 (over z, y), space: 4 (over x, core).
Axes of the slice: x: 2, y: 2, z: 4, core: 2. Of those that a mesh axis runs over, the one named last changes fastest.
Arguments:
- sigma_real: float32 [8, 64, 128], P('space'), may hold values from 0.3 to 3
- sigma_imag: float32 [8, 64, 128], P('space'), may hold values from -0.5 to 0.5
- warm_fields: float32 [32, 2, 8, 64, 128], P('elec', None, 'space'), may hold values from -6 to 6
- locations: int32 [32], P('elec'), may hold values from 0 to 65535
- counts: int32 [8], P('elec'), may hold values from 1 to 48, 128 in all
- quads: int32 [8, 48, 4], P('elec'), may hold values from 0 to 31
Outputs:
- jacobian: bfloat16 [128, 2, 8, 64, 128], P('elec', None, 'space')
Inputs may be any that keep to these rules, and one draw needn't show every extreme that they name: The counts sum to 128; group h's measurements are its first counts[h] slots. `quads`: slots past a group's count are unused.
All inputs are finite; a program needn't handle non-finite values.
Results may differ from a plain program's by a relative error of at most 0.0072.
Values may be sent and summed in bfloat16 or wider, within the bound.
A program may use at most 128 MiB of HBM per device.

v0:
```python
import math
import jax
import jax.numpy as jnp
from jax import lax
from jax.sharding import PartitionSpec as P

MEASURE_ROWS_MEAN = 16
ITERS = 2
screen = 0.3
current = 4.0


def padded_2(cells, sides, width):
    for axis, dim in sides:
        count = lax.axis_size(axis)
        ends = count - 1
        head = lax.slice_in_dim(cells, 0, width, axis=dim)
        tail = lax.slice_in_dim(cells, cells.shape[dim] - width, cells.shape[dim], axis=dim)
        cells = jnp.concatenate(
            [
                lax.ppermute(tail, axis, [(i, (i + 1) % count) for i in range(ends)]),
                cells,
                lax.ppermute(head, axis, [((i + 1) % count, i) for i in range(ends)]),
            ],
            axis=dim,
        )
    return cells


def relax_weights(count):
    spread_half = 6.0 / (6.0 + screen)
    return [
        1.0 / (1.0 + spread_half * math.cos(math.pi * (2 * k + 1) / (2 * count)))
        for k in range(count)
    ]


def gradients_of(padded_potential):
    values = padded_potential.astype(jnp.float32)
    interior = values[:, :, 1:-1]
    grad_x = (values[:, :, 2:] - values[:, :, :-2]) * 0.5
    side_pad = jnp.pad(interior, ((0, 0), (0, 0), (0, 0), (1, 1), (1, 1)))
    grad_y = (side_pad[:, :, :, 2:, 1:-1] - side_pad[:, :, :, :-2, 1:-1]) * 0.5
    grad_z = (side_pad[:, :, :, 1:-1, 2:] - side_pad[:, :, :, 1:-1, :-2]) * 0.5
    return jnp.stack([grad_x, grad_y, grad_z], axis=2).astype(jnp.bfloat16)


def per_device(sigma_real, sigma_imag, warm_fields, locations, counts, quads):
    group_width, cells_along_y, cells_along_z = sigma_real.shape
    slab = lax.axis_index("space")
    x_global = slab * group_width + lax.broadcasted_iota(
        jnp.int32, (group_width, cells_along_y, cells_along_z), 0
    )
    y_index = lax.broadcasted_iota(jnp.int32, (group_width, cells_along_y, cells_along_z), 1)
    z_index = lax.broadcasted_iota(jnp.int32, (group_width, cells_along_y, cells_along_z), 2)
    flat_index = (x_global * cells_along_y + y_index) * cells_along_z + z_index
    inverse = 1.0 / ((6.0 + screen) * (sigma_real * sigma_real + sigma_imag * sigma_imag))
    strength = jnp.where(
        flat_index[None] == locations[:, None, None, None], jnp.float32(current), jnp.float32(0.0)
    )
    source = jnp.stack(
        [strength * sigma_real * inverse, -(strength * sigma_imag * inverse)], axis=1
    )
    weights = relax_weights(ITERS)
    field = warm_fields
    for iteration in range(ITERS):
        padded = padded_2(field, (("space", 2),), 1)
        interior = padded[:, :, 1:-1]
        side_pad = jnp.pad(interior, ((0, 0), (0, 0), (0, 0), (1, 1), (1, 1)))
        total = padded[:, :, 2:] + padded[:, :, :-2]
        total = total + side_pad[:, :, :, 2:, 1:-1] + side_pad[:, :, :, :-2, 1:-1]
        total = total + side_pad[:, :, :, 1:-1, 2:] + side_pad[:, :, :, 1:-1, :-2]
        field = field + weights[iteration] * (source - field + total / (6.0 + screen))
    potential = field.astype(jnp.bfloat16)
    own_grads = gradients_of(padded_2(potential, (("space", 2),), 1))
    gradient_table = lax.all_gather(own_grads, "elec", axis=0, tiled=True)
    all_counts, all_quads = (
        lax.all_gather(counts, "elec", axis=0, tiled=True),
        lax.all_gather(quads, "elec", axis=0, tiled=True),
    )
    capacity = all_quads.shape[1]
    ends = jnp.cumsum(all_counts)
    starts = ends - all_counts
    measure_group = lax.axis_index("elec")
    row_indices = measure_group * MEASURE_ROWS_MEAN + jnp.arange(MEASURE_ROWS_MEAN, dtype=jnp.int32)
    owners = jnp.sum((ends[None, :] <= row_indices[:, None]).astype(jnp.int32), axis=1)
    slot_ids = row_indices - starts[owners]
    chosen = all_quads.reshape(-1, 4)[owners * capacity + slot_ids]
    electrodes = gradient_table.shape[0]
    electrode_ids = jnp.arange(electrodes, dtype=jnp.int32)[None, :]
    select_source = (chosen[:, 0:1] == electrode_ids).astype(jnp.float32) - (
        chosen[:, 1:2] == electrode_ids
    ).astype(jnp.float32)
    select_probe = (chosen[:, 2:3] == electrode_ids).astype(jnp.float32) - (
        chosen[:, 3:4] == electrode_ids
    ).astype(jnp.float32)
    selector = jnp.concatenate([select_source, select_probe], axis=0).astype(jnp.bfloat16)
    field_products = jnp.dot(
        selector, gradient_table.reshape(electrodes, -1), preferred_element_type=jnp.float32
    )
    field_products = field_products.reshape(
        2, MEASURE_ROWS_MEAN, 2, 3, group_width, cells_along_y, cells_along_z
    )
    pair_source = field_products[0]
    pair_probe = field_products[1]
    dot_real = jnp.sum(
        pair_source[:, 0] * pair_probe[:, 0] - pair_source[:, 1] * pair_probe[:, 1], axis=1
    )
    dot_imag = jnp.sum(
        pair_source[:, 0] * pair_probe[:, 1] + pair_source[:, 1] * pair_probe[:, 0], axis=1
    )
    part_real = -(sigma_real * dot_real - sigma_imag * dot_imag)
    part_imag = -(sigma_real * dot_imag + sigma_imag * dot_real)
    return jnp.stack([part_real, part_imag], axis=1).astype(jnp.bfloat16)


def solution(mesh):
    in_specs = (
        P("space", None, None),
        P("space", None, None),
        P("elec", None, "space", None, None),
        P("elec"),
        P("elec"),
        P("elec", None, None),
    )
    out_specs = P("elec", None, "space", None, None)
    return jax.shard_map(
        per_device, mesh=mesh, in_specs=in_specs, out_specs=out_specs, check_vma=False
    )
```

profile of v0, /device:TPU:0, one launch (start us, length us, event | category | flops | bytes accessed | tf_op | source)
XLA Modules:
  0.0 178.6 jit_solution(6735330070216509067)
XLA Ops:
  6.5 1.1 fusion.50
  7.6 1.3 collective-permute-start
  8.9 3.0 %collective-permute-start.1 = (f32[4,2,1,64,128]{4,3,2,1,0:T(8,128)S(1)}, f32[4,2,1,64,128]{4,3,2,1,0:T(8,128)S(1)}, u32[]{:S(2)}, u32[]{:S(2)}) collective-permute-start(f32[4,2,1,64,128]{4,3,2,1,0:T(8,128)S(1)} %get-tuple-element.22), channel_id=1, source_target_pairs={{0,1},{1,2},{2,3},{4,5},{5,6},{6,7},{8,9},{9,10},{10,11},{12,13},{... | collective-permute-start | bytes 786440 | tf_op jit(solution)/shard_map/ppermute | solution.py:21
  12.0 0.9 multiply_divide_fusion
  13.0 1.0 fusion.36
  14.0 3.0 %fusion.16 = f32[4,2,2,64,128]{4,3,2,1,0:T(8,128)S(1)} fusion(f32[4,2,2,64,128]{4,3,2,1,0:T(8,128)} %param.8, f32[4,2,1,64,128]{4,3,2,1,0:T(8,128)S(1)} %collective-permute-done.1, f32[4,2,1,64,128]{4,3,2,1,0:T(8,128)S(1)} %collective-permute-done, f32[4,1,2,64,128]{4,3,2,1,0:T(8,128)S(1)} %get-tuple-element.26, f32[4,1,2,64,128]{4,3,2,1,0:T(8,128)S(1)} %get-tuple-element.25), kind=kLoop, calls=%fused_computation.40 | loop fusion | flops 1703936 | bytes 2097152 | tf_op jit(solution)/shard_map/add | solution.py:73
  17.1 1.3 collective-permute-start.2
  18.4 6.3 %collective-permute-start.3 = (f32[4,2,1,64,128]{4,3,2,1,0:T(8,128)S(1)}, f32[4,2,1,64,128]{4,3,2,1,0:T(8,128)S(1)}, u32[]{:S(2)}, u32[]{:S(2)}) collective-permute-start(f32[4,2,1,64,128]{4,3,2,1,0:T(8,128)S(1)} %get-tuple-element.20), channel_id=1, source_target_pairs={{0,1},{1,2},{2,3},{4,5},{5,6},{6,7},{8,9},{9,10},{10,11},{12,13},{... | collective-permute-start | bytes 786440 | tf_op jit(solution)/shard_map/ppermute | solution.py:21
  24.8 1.1 collective-permute-done.3
  26.4 6.5 %collective-permute-start.4 = (bf16[4,2,1,64,128]{4,3,2,1,0:T(8,128)(2,1)S(1)}, bf16[4,2,1,64,128]{4,3,2,1,0:T(8,128)(2,1)S(1)}, u32[]{:S(2)}, u32[]{:S(2)}) collective-permute-start(bf16[4,2,1,64,128]{4,3,2,1,0:T(8,128)(2,1)S(1)} %get-tuple-element.23), channel_id=1, source_target_pairs={{0,1},{1,2},{2,3},{4,5},{5,6},{6,7},{8,9},{9,10},{10,11},{12,13},{... | collective-permute-start | bytes 393224 | tf_op jit(solution)/shard_map/ppermute | solution.py:21
  32.9 1.3 collective-permute-start.5
  34.2 3.9 %collective-permute-done.5 = bf16[4,2,1,64,128]{4,3,2,1,0:T(8,128)(2,1)S(1)} collective-permute-done((bf16[4,2,1,64,128]{4,3,2,1,0:T(8,128)(2,1)S(1)}, bf16[4,2,1,64,128]{4,3,2,1,0:T(8,128)(2,1)S(1)}, u32[]{:S(2)}, u32[]{:S(2)}) %collective-permute-start.5) | collective-permute-done | bytes 131104 | tf_op jit(solution)/shard_map/ppermute | solution.py:23
  38.7 1.0 pad_maximum_fusion.1
  41.0 0.7 dynamic-update-slice
  41.7 11.6 %all-reduce.3 = s32[8]{0:T(128)S(1)} all-reduce(s32[8]{0:T(128)S(1)} %dynamic-update-slice), channel_id=1, replica_groups=mesh['elec'=8,'space'=4] {'elec'}, use_global_device_ids=true, to_apply=%add.3 | all-reduce | flops 8 | bytes 64
  53.5 26.8 %all_gather.9 = s32[8,48,4]{1,2,0:T(4,128)S(1)} all-gather(s32[1,48,4]{1,2,0:T(4,128)S(1)} %copy-done.2), channel_id=1, replica_groups=mesh['elec'=8,'space'=4] {'elec'}, dimensions={0}, use_global_device_ids=true | all-gather | bytes 6912 | tf_op jit(solution)/shard_map/all_gather | solution.py:79
  82.0 60.7 %all-gather.2.cloned.1.call-done = bf16[32,2,3,2,64,128]{5,4,3,1,0,2:T(8,128)(2,1)} async-done(((bf16[4,2,3,2,64,128]{5,4,3,1,0,2:T(8,128)(2,1)}), bf16[32,2,3,2,64,128]{5,4,3,1,0,2:T(8,128)(2,1)}) %all-gather.2.cloned.1.call-update) | async-done | bytes 6291472 | tf_op jit(solution)/shard_map/all_gather | solution.py:76
  142.7 4.3 %copy.13 = bf16[32,2,3,2,64,128]{5,4,3,2,1,0:T(8,128)(2,1)S(1)} copy(bf16[32,2,3,2,64,128]{5,4,3,1,0,2:T(8,128)(2,1)} %all-gather.2.cloned.1.call-done) | data formatting | bytes 12582912 | tf_op jit(solution)/shard_map/all_gather | solution.py:76
  147.0 8.3 %fusion = f32[32,98304]{1,0:T(8,128)} fusion(bf16[4,8,768,128]{3,2,1,0:T(8,128)(2,1)S(1)} %bitcast.61, bf16[16,32]{1,0:T(8,128)(2,1)S(1)} %get-tuple-element.27, bf16[16,32]{1,0:T(8,128)(2,1)S(1)} %get-tuple-element.28), kind=kOutput, calls=%fused_computation.2 | convolution fusion | flops 201330688 | bytes 18876416 | tf_op jit(solution)/shard_map/dot_general | solution.py:98
  155.3 8.0 %slice_bitcast_fusion.1 = (f32[2,8,768,128]{3,1,2,0:T(8,128)}, f32[2,8,768,128]{3,1,2,0:T(8,128)S(1)}) fusion(f32[32,98304]{1,0:T(8,128)} %fusion), kind=kLoop, calls=%fused_computation.6 | loop fusion | bytes 25165824
  163.4 4.0 %copy.15 = f32[2,8,768,128]{3,2,1,0:T(8,128)S(1)} copy(f32[2,8,768,128]{3,1,2,0:T(8,128)} %get-tuple-element.11) | data formatting | bytes 12582912
  167.4 1.2 copy.16
  168.6 1.7 subtract_reduce_fusion
  170.7 1.1 pad_maximum_fusion
  (38 shorter events, 4.1 us)
Async XLA Ops:
  6.5 136.2 %all-gather.2.cloned.1.call-start = ((), (), s32[]{:S(2)}) async-start(), calls=%async_computation | async-start | bytes 7077888 | tf_op jit(solution)/shard_map/all_gather | solution.py:76
  7.6 6.4 %collective-permute-start = (f32[4,2,1,64,128]{4,3,2,1,0:T(8,128)S(1)}, f32[4,2,1,64,128]{4,3,2,1,0:T(8,128)S(1)}, u32[]{:S(2)}, u32[]{:S(2)}) collective-permute-start(f32[4,2,1,64,128]{4,3,2,1,0:T(8,128)S(1)} %get-tuple-element.21), channel_id=1, source_target_pairs={{1,0},{2,1},{3,2},{5,4},{6,5},{7,6},{9,8},{10,9},{11,10},{13,12},{... | collective-permute-start | bytes 786440 | tf_op jit(solution)/shard_map/ppermute | solution.py:23
  8.9 5.1 %collective-permute-start.1 = (f32[4,2,1,64,128]{4,3,2,1,0:T(8,128)S(1)}, f32[4,2,1,64,128]{4,3,2,1,0:T(8,128)S(1)}, u32[]{:S(2)}, u32[]{:S(2)}) collective-permute-start(f32[4,2,1,64,128]{4,3,2,1,0:T(8,128)S(1)} %get-tuple-element.22), channel_id=1, source_target_pairs={{0,1},{1,2},{2,3},{4,5},{5,6},{6,7},{8,9},{9,10},{10,11},{12,13},{... | collective-permute-start | bytes 786440 | tf_op jit(solution)/shard_map/ppermute | solution.py:21
  14.0 26.4 %copy-start.3 = (u32[32]{0:T(128)S(1)}, u32[32]{0:T(128)}, u32[]{:S(2)}) copy-start(u32[32]{0:T(128)} %constant.62) | copy-start | bytes 388
  14.0 39.4 %copy-start.2 = (s32[1,48,4]{1,2,0:T(4,128)S(1)}, s32[1,48,4]{1,2,0:T(4,128)}, u32[]{:S(2)}) copy-start(s32[1,48,4]{1,2,0:T(4,128)} %param.11) | copy-start | bytes 2308
  17.1 7.6 %collective-permute-start.2 = (f32[4,2,1,64,128]{4,3,2,1,0:T(8,128)S(1)}, f32[4,2,1,64,128]{4,3,2,1,0:T(8,128)S(1)}, u32[]{:S(2)}, u32[]{:S(2)}) collective-permute-start(f32[4,2,1,64,128]{4,3,2,1,0:T(8,128)S(1)} %get-tuple-element.19), channel_id=1, source_target_pairs={{1,0},{2,1},{3,2},{5,4},{6,5},{7,6},{9,8},{10,9},{11,10},{13,12},{... | collective-permute-start | bytes 786440 | tf_op jit(solution)/shard_map/ppermute | solution.py:23
  18.4 7.5 %collective-permute-start.3 = (f32[4,2,1,64,128]{4,3,2,1,0:T(8,128)S(1)}, f32[4,2,1,64,128]{4,3,2,1,0:T(8,128)S(1)}, u32[]{:S(2)}, u32[]{:S(2)}) collective-permute-start(f32[4,2,1,64,128]{4,3,2,1,0:T(8,128)S(1)} %get-tuple-element.20), channel_id=1, source_target_pairs={{0,1},{1,2},{2,3},{4,5},{5,6},{6,7},{8,9},{9,10},{10,11},{12,13},{... | collective-permute-start | bytes 786440 | tf_op jit(solution)/shard_map/ppermute | solution.py:21
  26.4 7.9 %collective-permute-start.4 = (bf16[4,2,1,64,128]{4,3,2,1,0:T(8,128)(2,1)S(1)}, bf16[4,2,1,64,128]{4,3,2,1,0:T(8,128)(2,1)S(1)}, u32[]{:S(2)}, u32[]{:S(2)}) collective-permute-start(bf16[4,2,1,64,128]{4,3,2,1,0:T(8,128)(2,1)S(1)} %get-tuple-element.23), channel_id=1, source_target_pairs={{0,1},{1,2},{2,3},{4,5},{5,6},{6,7},{8,9},{9,10},{10,11},{12,13},{... | collective-permute-start | bytes 393224 | tf_op jit(solution)/shard_map/ppermute | solution.py:21
  32.9 5.2 %collective-permute-start.5 = (bf16[4,2,1,64,128]{4,3,2,1,0:T(8,128)(2,1)S(1)}, bf16[4,2,1,64,128]{4,3,2,1,0:T(8,128)(2,1)S(1)}, u32[]{:S(2)}, u32[]{:S(2)}) collective-permute-start(bf16[4,2,1,64,128]{4,3,2,1,0:T(8,128)(2,1)S(1)} %get-tuple-element.24), channel_id=1, source_target_pairs={{1,0},{2,1},{3,2},{5,4},{6,5},{7,6},{9,8},{10,9},{11,10},{13,12},{... | collective-permute-start | bytes 393224 | tf_op jit(solution)/shard_map/ppermute | solution.py:23
  168.6 1.7 copy-start
  168.6 1.7 copy-start.1
Sparse Core Ops, SparseCore 0:
  39.8 102.8 all-gather.1
where the time goes:
time: 179 us
  waiting for transfers between devices  65.8 us (37%)
  blocking collectives  38.4 us (21%)
  local copies, waits for them, and re-layouts  21.5 us (12%)
  starting transfers between devices  19.8 us (11%)
  between operations  14.3 us (8%)
  other arithmetic  10.5 us (6%)
  matrix products  8.32 us (5%)
    all_gather x1, waiting for transfers between devices, per_device(): gradient_table = lax.all_gather(own_grads, 'elec', axis=0, tiled=True)  60.7 us
    all_gather x1, blocking collectives, per_device(): lax.all_gather(quads, 'elec', axis=0, tiled=True)  26.8 us
    ppermute x3, starting transfers between devices, padded_2(): lax.ppermute(tail, axis, [(i, (i + 1) % count) for i in range(ends)])  15.9 us
    unnamed x14, local copies, waits for them, and re-layouts  14.5 us
    unnamed x1, blocking collectives  11.6 us
    dot_general x1, matrix products, per_device(): jnp.dot(selector, gradient_table.reshape(electrodes, -1), preferred_eleme...  8.32 us
    all_gather x1, local copies, waits for them, and re-layouts, per_device(): gradient_table = lax.all_gather(own_grads, 'elec', axis=0, tiled=True)  4.28 us
    ppermute x3, waiting for transfers between devices, padded_2(): lax.ppermute(head, axis, [((i + 1) % count, i) for i in range(ends)])  3.92 us
  transfers between devices with their start and end apart: 7, of which 3 were waited for; matrix products, arithmetic and copies ran while one was open for 3% of the time, Pallas kernels for 0%

commit v1 on v0

--- a/solution.py
+++ b/solution.py
@@ -8,6 +8,19 @@
 ITERS = 2
 screen = 0.3
 current = 4.0
+
+
+def turn_stops_all_for(packet):
+    how_many = jax.lax.axis_size("elec")
+    near = sorted(((w, (w + 1) % how_many) for w in range(how_many)))
+    earlier = packet
+    stack_in = [earlier]
+    for src_i in range(1, how_many):
+        earlier = jax.lax.ppermute(earlier, axis_name="elec", perm=near)
+        stack_in.insert(0, earlier)
+    return jnp.roll(
+        jnp.concatenate(stack_in, 0), (jax.lax.axis_index("elec") + 1) * packet.shape[0], 0
+    )
 
 
 def padded_2(cells, sides, width):
@@ -73,7 +86,7 @@
         field = field + weights[iteration] * (source - field + total / (6.0 + screen))
     potential = field.astype(jnp.bfloat16)
     own_grads = gradients_of(padded_2(potential, (("space", 2),), 1))
-    gradient_table = lax.all_gather(own_grads, "elec", axis=0, tiled=True)
+    gradient_table = turn_stops_all_for(own_grads)
     all_counts, all_quads = (
         lax.all_gather(counts, "elec", axis=0, tiled=True),
         lax.all_gather(quads, "elec", axis=0, tiled=True),

time: 179 us -> 263 us (1.47)
  waiting for transfers between devices: 65.8 us -> 124 us
  local copies, waits for them, and re-layouts: 21.5 us -> 49 us
  between operations: 14.3 us -> 0.98 us
  blocking collectives: 38.4 us -> 45 us
  starting transfers between devices: 19.8 us -> 23.6 us
    ppermute x0 -> x7, waiting for transfers between devices: none -> 119 us  [turn_stops_all_for(): earlier = jax.lax.ppermute(earlier, axis_name='elec', perm=near)]
    all_gather x1 -> x0, waiting for transfers between devices: 60.7 us -> none  [per_device(): gradient_table = lax.all_gather(own_grads, 'elec', axis=0, tiled=True)]
    unnamed x14 -> x28, local copies, waits for them, and re-layouts: 14.5 us -> 39.1 us
    dynamic_slice x0 -> x2, local copies, waits for them, and re-layouts: none -> 7.17 us  [turn_stops_all_for(): jnp.roll(jnp.concatenate(stack_in, 0), (jax.lax.axis_index('elec') + 1) *...]
    all_gather x1 -> x0, local copies, waits for them, and re-layouts: 4.28 us -> none  [per_device(): gradient_table = lax.all_gather(own_grads, 'elec', axis=0, tiled=True)]
    all_gather x1, blocking collectives: 26.8 us -> 30.8 us  [per_device(): lax.all_gather(quads, 'elec', axis=0, tiled=True)]
    ppermute x0 -> x7, starting transfers between devices: none -> 3.83 us  [turn_stops_all_for(): earlier = jax.lax.ppermute(earlier, axis_name='elec', perm=near)]
  transfers between devices with their start and end apart: 7 -> 13, of which waited for: 3 -> 8; matrix products, arithmetic and copies ran while one was open for 3% -> 2% of each run, Pallas kernels for 0% -> 0%
where the time goes in v1:
time: 263 us; the launch traced here: 262 us
  waiting for transfers between devices  124 us (47%)
  local copies, waits for them, and re-layouts  49 us (19%)
  blocking collectives  45 us (17%)
  starting transfers between devices  23.6 us (9%)
  other arithmetic  11.7 us (4%)
  matrix products  8.32 us (3%)
    ppermute x7, waiting for transfers between devices, turn_stops_all_for(): earlier = jax.lax.ppermute(earlier, axis_name='elec', perm=near)  119 us
    unnamed x28, local copies, waits for them, and re-layouts  39.1 us
    all_gather x1, blocking collectives, per_device(): lax.all_gather(quads, 'elec', axis=0, tiled=True)  30.8 us
    ppermute x3, starting transfers between devices, padded_2(): lax.ppermute(tail, axis, [(i, (i + 1) % count) for i in range(ends)])  15.9 us
    unnamed x1, blocking collectives  14.2 us
    dot_general x1, matrix products, per_device(): jnp.dot(selector, gradient_table.reshape(electrodes, -1), preferred_eleme...  8.32 us
    dynamic_slice x2, local copies, waits for them, and re-layouts, turn_stops_all_for(): jnp.roll(jnp.concatenate(stack_in, 0), (jax.lax.axis_index('elec') + 1) *...  7.17 us
  transfers between devices with their start and end apart: 13, of which 8 were waited for; matrix products, arithmetic and copies ran while one was open for 2% of the time, Pallas kernels for 0%

profile of v1, /device:TPU:0, one launch (start us, length us, event | category | flops | bytes accessed | tf_op | source)
XLA Modules:
  0.0 262.4 jit_solution(2402827462591655856)
XLA Ops:
  2.4 3.0 %collective-permute-start.1 = (f32[4,2,1,64,128]{4,3,2,1,0:T(8,128)S(1)}, f32[4,2,1,64,128]{4,3,2,1,0:T(8,128)S(1)}, u32[]{:S(2)}, u32[]{:S(2)}) collective-permute-start(f32[4,2,1,64,128]{4,3,2,1,0:T(8,128)S(1)} %get-tuple-element.22), channel_id=1, source_target_pairs={{0,1},{1,2},{2,3},{4,5},{5,6},{6,7},{8,9},{9,10},{10,11},{12,13},{... | collective-permute-start | bytes 786440 | tf_op jit(solution)/shard_map/ppermute | solution.py:34
  7.5 3.0 %fusion.16 = f32[4,2,2,64,128]{4,3,2,1,0:T(8,128)S(1)} fusion(f32[4,2,2,64,128]{4,3,2,1,0:T(8,128)} %param.8, f32[4,2,1,64,128]{4,3,2,1,0:T(8,128)S(1)} %collective-permute-done.1, f32[4,2,1,64,128]{4,3,2,1,0:T(8,128)S(1)} %collective-permute-done, f32[4,1,2,64,128]{4,3,2,1,0:T(8,128)S(1)} %get-tuple-element.26, f32[4,1,2,64,128]{4,3,2,1,0:T(8,128)S(1)} %get-tuple-element.25), kind=kLoop, calls=%fused_computation.40 | loop fusion | flops 1703936 | bytes 2097152 | tf_op jit(solution)/shard_map/add | solution.py:86
  11.9 6.3 %collective-permute-start.3 = (f32[4,2,1,64,128]{4,3,2,1,0:T(8,128)S(1)}, f32[4,2,1,64,128]{4,3,2,1,0:T(8,128)S(1)}, u32[]{:S(2)}, u32[]{:S(2)}) collective-permute-start(f32[4,2,1,64,128]{4,3,2,1,0:T(8,128)S(1)} %get-tuple-element.20), channel_id=1, source_target_pairs={{0,1},{1,2},{2,3},{4,5},{5,6},{6,7},{8,9},{9,10},{10,11},{12,13},{... | collective-permute-start | bytes 786440 | tf_op jit(solution)/shard_map/ppermute | solution.py:34
  19.8 6.5 %collective-permute-start.4 = (bf16[4,2,1,64,128]{4,3,2,1,0:T(8,128)(2,1)S(1)}, bf16[4,2,1,64,128]{4,3,2,1,0:T(8,128)(2,1)S(1)}, u32[]{:S(2)}, u32[]{:S(2)}) collective-permute-start(bf16[4,2,1,64,128]{4,3,2,1,0:T(8,128)(2,1)S(1)} %get-tuple-element.23), channel_id=1, source_target_pairs={{0,1},{1,2},{2,3},{4,5},{5,6},{6,7},{8,9},{9,10},{10,11},{12,13},{... | collective-permute-start | bytes 393224 | tf_op jit(solution)/shard_map/ppermute | solution.py:34
  27.7 3.9 %collective-permute-done.5 = bf16[4,2,1,64,128]{4,3,2,1,0:T(8,128)(2,1)S(1)} collective-permute-done((bf16[4,2,1,64,128]{4,3,2,1,0:T(8,128)(2,1)S(1)}, bf16[4,2,1,64,128]{4,3,2,1,0:T(8,128)(2,1)S(1)}, u32[]{:S(2)}, u32[]{:S(2)}) %collective-permute-start.5) | collective-permute-done | bytes 131104 | tf_op jit(solution)/shard_map/ppermute | solution.py:36
  33.9 18.8 %collective-permute-done.6 = bf16[4,2,3,2,64,128]{5,4,3,1,0,2:T(8,128)(2,1)S(1)} collective-permute-done((bf16[4,2,3,2,64,128]{5,4,3,1,0,2:T(8,128)(2,1)S(1)}, bf16[4,2,3,2,64,128]{5,4,3,1,0,2:T(8,128)(2,1)S(1)}, u32[]{:S(2)}, u32[]{:S(2)}) %collective-permute-start.6) | collective-permute-done | bytes 786464 | tf_op jit(solution)/shard_map/ppermute | solution.py:19
  52.7 21.4 %collective-permute-done.7 = bf16[4,2,3,2,64,128]{5,4,3,1,0,2:T(8,128)(2,1)S(1)} collective-permute-done((bf16[4,2,3,2,64,128]{5,4,3,1,0,2:T(8,128)(2,1)S(1)}, bf16[4,2,3,2,64,128]{5,4,3,1,0,2:T(8,128)(2,1)S(1)}, u32[]{:S(2)}, u32[]{:S(2)}) %collective-permute-start.7) | collective-permute-done | bytes 786464 | tf_op jit(solution)/shard_map/ppermute | solution.py:19
  74.2 22.6 %collective-permute-done.8 = bf16[4,2,3,2,64,128]{5,4,3,1,0,2:T(8,128)(2,1)S(1)} collective-permute-done((bf16[4,2,3,2,64,128]{5,4,3,1,0,2:T(8,128)(2,1)S(1)}, bf16[4,2,3,2,64,128]{5,4,3,1,0,2:T(8,128)(2,1)S(1)}, u32[]{:S(2)}, u32[]{:S(2)}) %collective-permute-start.8) | collective-permute-done | bytes 786464 | tf_op jit(solution)/shard_map/ppermute | solution.py:19
  96.8 22.5 %collective-permute-done.9 = bf16[4,2,3,2,64,128]{5,4,3,1,0,2:T(8,128)(2,1)} collective-permute-done((bf16[4,2,3,2,64,128]{5,4,3,1,0,2:T(8,128)(2,1)S(1)}, bf16[4,2,3,2,64,128]{5,4,3,1,0,2:T(8,128)(2,1)}, u32[]{:S(2)}, u32[]{:S(2)}) %collective-permute-start.9) | collective-permute-done | bytes 786464 | tf_op jit(solution)/shard_map/ppermute | solution.py:19
  119.3 21.9 %collective-permute-done.10 = bf16[4,2,3,2,64,128]{5,4,3,1,0,2:T(8,128)(2,1)} collective-permute-done((bf16[4,2,3,2,64,128]{5,4,3,1,0,2:T(8,128)(2,1)}, bf16[4,2,3,2,64,128]{5,4,3,1,0,2:T(8,128)(2,1)}, u32[]{:S(2)}, u32[]{:S(2)}) %collective-permute-start.10) | collective-permute-done | bytes 786464 | tf_op jit(solution)/shard_map/ppermute | solution.py:19
  143.3 14.2 %all-reduce.3 = s32[8]{0:T(128)S(1)} all-reduce(s32[8]{0:T(128)S(1)} %dynamic-update-slice), channel_id=1, replica_groups=mesh['elec'=8,'space'=4] {'elec'}, use_global_device_ids=true, to_apply=%add.3 | all-reduce | flops 8 | bytes 64
  157.6 30.8 %all_gather.6 = s32[8,48,4]{1,2,0:T(4,128)S(1)} all-gather(s32[1,48,4]{1,2,0:T(4,128)S(1)} %copy-done.2), channel_id=1, replica_groups=mesh['elec'=8,'space'=4] {'elec'}, dimensions={0}, use_global_device_ids=true | all-gather | bytes 6912 | tf_op jit(solution)/shard_map/all_gather | solution.py:92
  188.6 2.2 collective-permute-start.12
  192.5 11.3 %collective-permute-done.12 = bf16[4,2,3,2,64,128]{5,4,3,1,0,2:T(8,128)(2,1)} collective-permute-done((bf16[4,2,3,2,64,128]{5,4,3,1,0,2:T(8,128)(2,1)}, bf16[4,2,3,2,64,128]{5,4,3,1,0,2:T(8,128)(2,1)}, u32[]{:S(2)}, u32[]{:S(2)}) %collective-permute-start.12) | collective-permute-done | bytes 786464 | tf_op jit(solution)/shard_map/ppermute | solution.py:19
  203.8 2.3 constant_dynamic-update-slice_fusion.15
  210.6 2.3 constant_dynamic-update-slice_fusion.12
  217.1 2.3 constant_dynamic-update-slice_fusion.7
  219.4 2.3 constant_dynamic-update-slice_fusion.6
  221.6 2.3 constant_dynamic-update-slice_fusion.5
  230.3 4.3 %constant_dynamic-slice_fusion = bf16[32,2,3,2,64,128]{5,4,3,1,0,2:T(8,128)(2,1)S(1)} fusion(bf16[64,2,3,2,64,128]{5,4,3,1,0,2:T(8,128)(2,1)} %constant_dynamic-update-slice_fusion, s32[]{:T(128)S(6)} %select_n.52), kind=kLoop, calls=%fused_computation.118 | loop fusion | bytes 12582916 | tf_op jit(solution)/shard_map/jit(_roll_dynamic)/dynamic_slice | solution.py:21
  234.6 2.9 %copy.13 = bf16[32,2,3,2,64,128]{5,4,3,2,1,0:T(8,128)(2,1)S(1)} copy(bf16[32,2,3,2,64,128]{5,4,3,1,0,2:T(8,128)(2,1)S(1)} %constant_dynamic-slice_fusion) | data formatting | bytes 12582912 | tf_op jit(solution)/shard_map/jit(_roll_dynamic)/dynamic_slice | solution.py:21
  237.5 8.3 %fusion = f32[32,98304]{1,0:T(8,128)} fusion(bf16[4,8,768,128]{3,2,1,0:T(8,128)(2,1)S(1)} %bitcast.61, bf16[16,32]{1,0:T(8,128)(2,1)S(1)} %get-tuple-element.27, bf16[16,32]{1,0:T(8,128)(2,1)S(1)} %get-tuple-element.28), kind=kOutput, calls=%fused_computation.2 | convolution fusion | flops 201330688 | bytes 18876416 | tf_op jit(solution)/shard_map/dot_general | solution.py:111
  245.8 8.0 %slice_bitcast_fusion.1 = (f32[2,8,768,128]{3,1,2,0:T(8,128)}, f32[2,8,768,128]{3,1,2,0:T(8,128)S(1)}) fusion(f32[32,98304]{1,0:T(8,128)} %fusion), kind=kLoop, calls=%fused_computation.6 | loop fusion | bytes 25165824
  253.8 4.2 %copy.15 = f32[2,8,768,128]{3,2,1,0:T(8,128)S(1)} copy(f32[2,8,768,128]{3,1,2,0:T(8,128)} %get-tuple-element.11) | data formatting | bytes 12582912
  (66 shorter events, 33.6 us)
Async XLA Ops:
  0.0 141.9 %copy-start.3 = (u32[32]{0:T(128)S(1)}, u32[32]{0:T(128)}, u32[]{:S(2)}) copy-start(u32[32]{0:T(128)} %constant.87) | copy-start | bytes 388
  0.0 157.6 %copy-start.2 = (s32[1,48,4]{1,2,0:T(4,128)S(1)}, s32[1,48,4]{1,2,0:T(4,128)}, u32[]{:S(2)}) copy-start(s32[1,48,4]{1,2,0:T(4,128)} %param.11) | copy-start | bytes 2308
  1.1 6.4 %collective-permute-start = (f32[4,2,1,64,128]{4,3,2,1,0:T(8,128)S(1)}, f32[4,2,1,64,128]{4,3,2,1,0:T(8,128)S(1)}, u32[]{:S(2)}, u32[]{:S(2)}) collective-permute-start(f32[4,2,1,64,128]{4,3,2,1,0:T(8,128)S(1)} %get-tuple-element.21), channel_id=1, source_target_pairs={{1,0},{2,1},{3,2},{5,4},{6,5},{7,6},{9,8},{10,9},{11,10},{13,12},{... | collective-permute-start | bytes 786440 | tf_op jit(solution)/shard_map/ppermute | solution.py:36
  2.4 5.1 %collective-permute-start.1 = (f32[4,2,1,64,128]{4,3,2,1,0:T(8,128)S(1)}, f32[4,2,1,64,128]{4,3,2,1,0:T(8,128)S(1)}, u32[]{:S(2)}, u32[]{:S(2)}) collective-permute-start(f32[4,2,1,64,128]{4,3,2,1,0:T(8,128)S(1)} %get-tuple-element.22), channel_id=1, source_target_pairs={{0,1},{1,2},{2,3},{4,5},{5,6},{6,7},{8,9},{9,10},{10,11},{12,13},{... | collective-permute-start | bytes 786440 | tf_op jit(solution)/shard_map/ppermute | solution.py:34
  10.6 7.7 %collective-permute-start.2 = (f32[4,2,1,64,128]{4,3,2,1,0:T(8,128)S(1)}, f32[4,2,1,64,128]{4,3,2,1,0:T(8,128)S(1)}, u32[]{:S(2)}, u32[]{:S(2)}) collective-permute-start(f32[4,2,1,64,128]{4,3,2,1,0:T(8,128)S(1)} %get-tuple-element.19), channel_id=1, source_target_pairs={{1,0},{2,1},{3,2},{5,4},{6,5},{7,6},{9,8},{10,9},{11,10},{13,12},{... | collective-permute-start | bytes 786440 | tf_op jit(solution)/shard_map/ppermute | solution.py:36
  11.9 7.5 %collective-permute-start.3 = (f32[4,2,1,64,128]{4,3,2,1,0:T(8,128)S(1)}, f32[4,2,1,64,128]{4,3,2,1,0:T(8,128)S(1)}, u32[]{:S(2)}, u32[]{:S(2)}) collective-permute-start(f32[4,2,1,64,128]{4,3,2,1,0:T(8,128)S(1)} %get-tuple-element.20), channel_id=1, source_target_pairs={{0,1},{1,2},{2,3},{4,5},{5,6},{6,7},{8,9},{9,10},{10,11},{12,13},{... | collective-permute-start | bytes 786440 | tf_op jit(solution)/shard_map/ppermute | solution.py:34
  19.8 7.9 %collective-permute-start.4 = (bf16[4,2,1,64,128]{4,3,2,1,0:T(8,128)(2,1)S(1)}, bf16[4,2,1,64,128]{4,3,2,1,0:T(8,128)(2,1)S(1)}, u32[]{:S(2)}, u32[]{:S(2)}) collective-permute-start(bf16[4,2,1,64,128]{4,3,2,1,0:T(8,128)(2,1)S(1)} %get-tuple-element.23), channel_id=1, source_target_pairs={{0,1},{1,2},{2,3},{4,5},{5,6},{6,7},{8,9},{9,10},{10,11},{12,13},{... | collective-permute-start | bytes 393224 | tf_op jit(solution)/shard_map/ppermute | solution.py:34
  26.4 5.2 %collective-permute-start.5 = (bf16[4,2,1,64,128]{4,3,2,1,0:T(8,128)(2,1)S(1)}, bf16[4,2,1,64,128]{4,3,2,1,0:T(8,128)(2,1)S(1)}, u32[]{:S(2)}, u32[]{:S(2)}) collective-permute-start(bf16[4,2,1,64,128]{4,3,2,1,0:T(8,128)(2,1)S(1)} %get-tuple-element.24), channel_id=1, source_target_pairs={{1,0},{2,1},{3,2},{5,4},{6,5},{7,6},{9,8},{10,9},{11,10},{13,12},{... | collective-permute-start | bytes 393224 | tf_op jit(solution)/shard_map/ppermute | solution.py:36
  32.3 20.4 %collective-permute-start.6 = (bf16[4,2,3,2,64,128]{5,4,3,1,0,2:T(8,128)(2,1)S(1)}, bf16[4,2,3,2,64,128]{5,4,3,1,0,2:T(8,128)(2,1)S(1)}, u32[]{:S(2)}, u32[]{:S(2)}) collective-permute-start(bf16[4,2,3,2,64,128]{5,4,3,1,0,2:T(8,128)(2,1)S(1)} %pad_maximum_fusion.1), channel_id=1, source_target_pairs={{0,4},{4,8},{8,12},{12,16},{16,20},{20,24},{24,28},{28,0},{1,5},{5... | collective-permute-start | bytes 2359304 | tf_op jit(solution)/shard_map/ppermute | solution.py:19
  52.7 21.4 %collective-permute-start.7 = (bf16[4,2,3,2,64,128]{5,4,3,1,0,2:T(8,128)(2,1)S(1)}, bf16[4,2,3,2,64,128]{5,4,3,1,0,2:T(8,128)(2,1)S(1)}, u32[]{:S(2)}, u32[]{:S(2)}) collective-permute-start(bf16[4,2,3,2,64,128]{5,4,3,1,0,2:T(8,128)(2,1)S(1)} %collective-permute-done.6), channel_id=1, source_target_pairs={{0,4},{4,8},{8,12},{12,16},{16,20},{20,24},{24,28},{28,0},{1,5},{5... | collective-permute-start | bytes 2359304 | tf_op jit(solution)/shard_map/ppermute | solution.py:19
  74.2 22.6 %collective-permute-start.8 = (bf16[4,2,3,2,64,128]{5,4,3,1,0,2:T(8,128)(2,1)S(1)}, bf16[4,2,3,2,64,128]{5,4,3,1,0,2:T(8,128)(2,1)S(1)}, u32[]{:S(2)}, u32[]{:S(2)}) collective-permute-start(bf16[4,2,3,2,64,128]{5,4,3,1,0,2:T(8,128)(2,1)S(1)} %collective-permute-done.7), channel_id=1, source_target_pairs={{0,4},{4,8},{8,12},{12,16},{16,20},{20,24},{24,28},{28,0},{1,5},{5... | collective-permute-start | bytes 2359304 | tf_op jit(solution)/shard_map/ppermute | solution.py:19
  96.8 22.5 %collective-permute-start.9 = (bf16[4,2,3,2,64,128]{5,4,3,1,0,2:T(8,128)(2,1)S(1)}, bf16[4,2,3,2,64,128]{5,4,3,1,0,2:T(8,128)(2,1)}, u32[]{:S(2)}, u32[]{:S(2)}) collective-permute-start(bf16[4,2,3,2,64,128]{5,4,3,1,0,2:T(8,128)(2,1)S(1)} %collective-permute-done.8), channel_id=1, source_target_pairs={{0,4},{4,8},{8,12},{12,16},{16,20},{20,24},{24,28},{28,0},{1,5},{5... | collective-permute-start | bytes 2359304 | tf_op jit(solution)/shard_map/ppermute | solution.py:19
  119.3 21.9 %collective-permute-start.10 = (bf16[4,2,3,2,64,128]{5,4,3,1,0,2:T(8,128)(2,1)}, bf16[4,2,3,2,64,128]{5,4,3,1,0,2:T(8,128)(2,1)}, u32[]{:S(2)}, u32[]{:S(2)}) collective-permute-start(bf16[4,2,3,2,64,128]{5,4,3,1,0,2:T(8,128)(2,1)} %collective-permute-done.9), channel_id=1, source_target_pairs={{0,4},{4,8},{8,12},{12,16},{16,20},{20,24},{24,28},{28,0},{1,5},{5... | collective-permute-start | bytes 2359304 | tf_op jit(solution)/shard_map/ppermute | solution.py:19
  141.3 47.3 %collective-permute-start.11 = (bf16[4,2,3,2,64,128]{5,4,3,1,0,2:T(8,128)(2,1)}, bf16[4,2,3,2,64,128]{5,4,3,1,0,2:T(8,128)(2,1)}, u32[]{:S(2)}, u32[]{:S(2)}) collective-permute-start(bf16[4,2,3,2,64,128]{5,4,3,1,0,2:T(8,128)(2,1)} %collective-permute-done.10), channel_id=1, source_target_pairs={{0,4},{4,8},{8,12},{12,16},{16,20},{20,24},{24,28},{28,0},{1,5},{5... | collective-permute-start | bytes 2359304 | tf_op jit(solution)/shard_map/ppermute | solution.py:19
  188.6 15.2 %collective-permute-start.12 = (bf16[4,2,3,2,64,128]{5,4,3,1,0,2:T(8,128)(2,1)}, bf16[4,2,3,2,64,128]{5,4,3,1,0,2:T(8,128)(2,1)}, u32[]{:S(2)}, u32[]{:S(2)}) collective-permute-start(bf16[4,2,3,2,64,128]{5,4,3,1,0,2:T(8,128)(2,1)} %collective-permute-done.11), channel_id=1, source_target_pairs={{0,4},{4,8},{8,12},{12,16},{16,20},{20,24},{24,28},{28,0},{1,5},{5... | collective-permute-start | bytes 2359304 | tf_op jit(solution)/shard_map/ppermute | solution.py:19
  258.0 2.9 %copy-start = (f32[2,64,128]{2,1,0:T(8,128)S(1)}, f32[2,64,128]{2,1,0:T(8,128)}, u32[]{:S(2)}) copy-start(f32[2,64,128]{2,1,0:T(8,128)} %param.7) | copy-start | bytes 196612
  258.0 2.9 %copy-start.1 = (f32[2,64,128]{2,1,0:T(8,128)S(1)}, f32[2,64,128]{2,1,0:T(8,128)}, u32[]{:S(2)}) copy-start(f32[2,64,128]{2,1,0:T(8,128)} %param.6) | copy-start | bytes 196612
